TPU v7x, 512 devices: a whole 4x4x16 slice. The times are simulated.
512 devices in a mesh: samp: 64 (over y_lo, z, core), snp: 8 (over x, y_hi).
Axes of the slice: x: 4, y: 4 (y_hi: 2, y_lo: 2; y = y_hi * 2 + y_lo), z: 16, core: 2. Of those that a mesh axis runs over, the one named last changes fastest.
Arguments:
- genotype: int32 [65536, 4096], P('samp', 'snp'), may hold values from 0 to 3, as said below
- basis: bfloat16 [4096, 40], P('snp'), may hold values from -6 to 6
Outputs:
- sample_scores: bfloat16 [65536, 40], P('samp')
- snp_block: float32 [4096, 40], P('snp')
Inputs may be any that keep to these rules, and one draw needn't show every extreme that they name: `genotype`: the value 3 marks a missing call; 0, 1 and 2 are dosages.
All inputs are finite; a program needn't handle non-finite values.
Results may differ from a plain program's by a relative error of at most 0.0065.
Values may be sent and summed in bfloat16 or wider, within the bound.
No kernel may reach another device: no remote copies, remote signals or barrier semaphores. Data moves between devices by JAX's collectives and lax.ppermute only.
A program may use at most 64 MiB of HBM per device.

v0:
```python
import jax
import jax.numpy as jnp
from jax import lax
from jax.sharding import PartitionSpec as P

ITERS = 2


def sent_to_all(shard, axis):
    copies = jnp.broadcast_to(shard, (lax.axis_size(axis), *shard.shape))
    return lax.all_to_all(copies, axis, split_axis=0, concat_axis=0, tiled=True)


def taken_together(shard, axis):
    return sent_to_all(shard, axis).sum(axis=0)


def together(arrays, axis):
    line, at, outs = (jnp.concatenate([a.reshape(-1) for a in arrays]), 0, [])
    total = taken_together(line, axis)
    for a in arrays:
        outs.append(total[at : at + a.size].reshape(a.shape))
        at += a.size
    return tuple(outs)


def of_everyone(shard, axis):
    everything = sent_to_all(shard, axis)
    return jnp.sum(everything.astype(jnp.float32), axis=0)


def rows_for(lines, peers):
    spare = -lines.shape[0] % peers
    if not spare:
        return lines
    return jnp.concatenate([lines, jnp.zeros((spare, *lines.shape[1:]), lines.dtype)])


def in_order(blocks, dim):
    dims = list(blocks.shape[1:])
    dims[dim] *= blocks.shape[0]
    return jnp.moveaxis(blocks, 0, dim).reshape(dims)


def gather_directly(shard, axis, dim):
    blocks = sent_to_all(shard, axis)
    return in_order(blocks, dim)


def cut_along(shard, dim, peers):
    before, after = (shard.shape[:dim], shard.shape[dim + 1 :])
    return jnp.moveaxis(shard.reshape(*before, peers, -1, *after), dim, 0)


def sent_and_summed(shard, axis, dim):
    blocks = cut_along(shard, dim, lax.axis_size(axis))
    arrived = lax.all_to_all(blocks, axis, split_axis=0, concat_axis=0, tiled=True)
    return arrived.astype(jnp.float32).sum(axis=0)


def total_of(shard, axes):
    lines = shard.reshape(-1, shard.shape[-1])
    padded = rows_for(lines, lax.axis_size(axes))
    whole = gather_directly(sent_and_summed(padded, axes, 0).astype(jnp.bfloat16), axes, 0)
    return lax.slice_in_dim(whole, 0, len(lines)).reshape(shard.shape).astype(jnp.float32)


def per_device(genotype, basis):
    observed = genotype < 3
    dosage = jnp.where(observed, genotype, 0).astype(jnp.float32)
    allele_sum, called = together(
        (jnp.sum(dosage, axis=0), jnp.sum(observed.astype(jnp.float32), axis=0)), "samp"
    )
    freq = (allele_sum + 1.0) / (2.0 * called + 2.0)
    scale = 1.0 / jnp.sqrt(2.0 * freq * (1.0 - freq))
    standard = jnp.where(observed, (dosage - 2.0 * freq) * scale, 0.0).astype(jnp.bfloat16)
    row_count = genotype.shape[0]
    total = row_count * lax.axis_size("samp")
    contract = (((0,), (0,)), ((), ()))
    block = basis
    for step in range(ITERS):
        scores = of_everyone(
            jnp.dot(standard, block, preferred_element_type=jnp.float32).astype(jnp.bfloat16), "snp"
        ).astype(jnp.float32)
        sample_scores = scores.astype(jnp.bfloat16)
        local = lax.dot_general(
            standard, sample_scores, contract, preferred_element_type=jnp.float32
        )
        snp_block = total_of(local.astype(jnp.bfloat16), "samp") / total
        block = snp_block.astype(jnp.bfloat16)
    return (sample_scores, snp_block)


def solution(mesh):
    placed = (P("samp", "snp"), P("snp", None))
    return jax.shard_map(
        per_device,
        mesh=mesh,
        in_specs=placed,
        out_specs=(P("samp", None), P("snp", None)),
        check_vma=False,
    )
```

profile of v0, /device:TPU:1, one launch (start us, length us, event | category | flops | bytes accessed | tf_op | source)
XLA Modules:
  0.0 156.8 jit_solution(5316181969101537312)
XLA Ops:
  0.7 2.2 %convert_reduce_fusion.1 = (f32[512]{0:T(512)S(1)}, f32[512]{0:T(512)S(1)}) fusion(s32[1024,512]{1,0:T(8,128)} %param.2), kind=kLoop, calls=%fused_computation.2 | loop fusion | flops 3144704 | bytes 2101248 | tf_op jit(solution)/shard_map/reduce_sum | solution.py:72
  2.8 0.1 broadcast_in_dim.26
  3.0 40.2 %all_to_all.36 = f32[64,1,1024]{2,1,0:T(1,128)S(1)} all-to-all(f32[64,1,1024]{2,1,0:T(1,128)S(1)} %broadcast_in_dim.26), channel_id=1, replica_groups=mesh['samp'=64,'snp'=8] {'samp'}, dimensions={0} | all-to-all | bytes 524288 | tf_op jit(solution)/shard_map/all_to_all | solution.py:11
  43.2 0.2 reduce_sum.77
  43.4 0.5 select_convert_fusion
  43.9 0.4 convolution_convert_fusion.1
  44.3 0.1 broadcast_in_dim.28
  44.4 18.7 %all_to_all.37 = bf16[8,1024,40]{1,2,0:T(8,128)(2,1)S(1)} all-to-all(bf16[8,1024,40]{1,2,0:T(8,128)(2,1)S(1)} %broadcast_in_dim.28), channel_id=1, replica_groups=mesh['samp'=64,'snp'=8] {'snp'}, dimensions={0} | all-to-all | bytes 1310720 | tf_op jit(solution)/shard_map/all_to_all | solution.py:11
  63.0 0.1 reduce_sum.78
  63.1 0.3 convolution_convert_fusion.3
  63.4 0.1 copy.19
  63.6 0.2 reshape.27
  63.7 19.1 %all_to_all.38 = bf16[64,2,160]{2,1,0:T(2,128)(2,1)S(1)} all-to-all(bf16[64,2,160]{2,1,0:T(2,128)(2,1)S(1)} %reshape.27), channel_id=1, replica_groups=mesh['samp'=64,'snp'=8] {'samp'}, dimensions={0} | all-to-all | bytes 81920 | tf_op jit(solution)/shard_map/all_to_all | solution.py:57
  82.8 0.1 reshape.28
  82.9 0.1 reduce_sum.79
  83.0 0.2 reshape.29
  83.2 18.3 %all_to_all.39 = bf16[64,2,160]{2,1,0:T(2,128)(2,1)S(1)} all-to-all(bf16[64,2,160]{2,1,0:T(2,128)(2,1)S(1)} %reshape.29), channel_id=1, replica_groups=mesh['samp'=64,'snp'=8] {'samp'}, dimensions={0} | all-to-all | bytes 81920 | tf_op jit(solution)/shard_map/all_to_all | solution.py:11
  101.5 0.1 reshape.30
  101.7 0.4 convolution_convert_fusion
  102.1 0.1 broadcast_in_dim.30
  102.2 14.1 %all_to_all.40 = bf16[8,1024,40]{1,2,0:T(8,128)(2,1)S(1)} all-to-all(bf16[8,1024,40]{1,2,0:T(8,128)(2,1)S(1)} %broadcast_in_dim.30), channel_id=1, replica_groups=mesh['samp'=64,'snp'=8] {'snp'}, dimensions={0} | all-to-all | bytes 1310720 | tf_op jit(solution)/shard_map/all_to_all | solution.py:11
  116.3 0.1 reduce_sum.80
  116.4 0.3 convolution_convert_fusion.2
  116.7 0.1 copy.20
  116.8 0.2 reshape.31
  117.0 20.1 %all_to_all.41 = bf16[64,2,160]{2,1,0:T(2,128)(2,1)S(1)} all-to-all(bf16[64,2,160]{2,1,0:T(2,128)(2,1)S(1)} %reshape.31), channel_id=1, replica_groups=mesh['samp'=64,'snp'=8] {'samp'}, dimensions={0} | all-to-all | bytes 81920 | tf_op jit(solution)/shard_map/all_to_all | solution.py:57
  137.1 0.1 reshape.32
  137.3 0.1 reduce_sum.81
  137.4 0.2 reshape.33
  137.5 18.3 %all_to_all.42 = bf16[64,2,160]{2,1,0:T(2,128)(2,1)S(1)} all-to-all(bf16[64,2,160]{2,1,0:T(2,128)(2,1)S(1)} %reshape.33), channel_id=1, replica_groups=mesh['samp'=64,'snp'=8] {'samp'}, dimensions={0} | all-to-all | bytes 81920 | tf_op jit(solution)/shard_map/all_to_all | solution.py:11
  155.9 0.1 reshape.34
  156.0 0.7 copy.21
  (12 shorter events, 0.1 us)
Async XLA Ops:
  0.6 43.3 %copy-start = (bf16[512,40]{0,1:T(8,128)(2,1)S(1)}, bf16[512,40]{0,1:T(8,128)(2,1)}, u32[]{:S(2)}) copy-start(bf16[512,40]{0,1:T(8,128)(2,1)} %param.3) | copy-start | bytes 122884
  0.6 42.8 %copy-start.1 = (s32[1024,512]{1,0:T(8,128)S(1)}, s32[1024,512]{1,0:T(8,128)}, u32[]{:S(2)}) copy-start(s32[1024,512]{1,0:T(8,128)} %param.2) | copy-start | bytes 6291460
  116.4 40.4 %copy-start.2 = (bf16[1024,40]{0,1:T(8,128)(2,1)}, bf16[1024,40]{0,1:T(8,128)(2,1)S(1)}, u32[]{:S(2)}) copy-start(bf16[1024,40]{0,1:T(8,128)(2,1)S(1)} %reduce_sum.80) | copy-start | bytes 245764
where the time goes:
time: 157 us
  blocking collectives  149 us (95%)
  other arithmetic  3.22 us (2%)
  local copies, waits for them, and re-layouts  2.51 us (2%)
    all_to_all x5, blocking collectives, sent_to_all(): return lax.all_to_all(copies, axis, split_axis=0, concat_axis=0, tiled=True)  110 us
    all_to_all x2, blocking collectives, sent_and_summed(): lax.all_to_all(blocks, axis, split_axis=0, concat_axis=0, tiled=True)  39.2 us

commit v1 on v0

v1 whole, which is shorter than its diff:
```python
import jax
import jax.numpy as jnp
from jax import lax
from jax.sharding import PartitionSpec as P

ITERS = 2
LANES = 128


def samp_groups(mesh):
    size = mesh.shape["samp"]
    depth = size // 4
    at = lambda y, z, c: (y * depth + z) * 2 + c
    level = [[at(y, z, c) for y in range(2) for c in range(2)] for z in range(depth)]
    column = [[at(y, z, c) for z in range(depth)] for y in range(2) for c in range(2)]
    return level, column


def exchange(blocks, axis, groups=None):
    return lax.all_to_all(
        blocks, axis, split_axis=0, concat_axis=0, tiled=True, axis_index_groups=groups
    )


def from_all(shard, axis, members, groups=None):
    return exchange(jnp.broadcast_to(shard, (members, *shard.shape)), axis, groups)


def solution(mesh):
    level, column = samp_groups(mesh)
    near, far = len(level[0]), len(column[0])
    peers = mesh.shape["snp"]

    def over_samples(counts):
        held = from_all(counts.astype(jnp.int16), "samp", near, level)
        part = jnp.sum(held.astype(jnp.int32), axis=0)
        held = from_all(part.astype(jnp.int16), "samp", far, column)
        return jnp.sum(held.astype(jnp.int32), axis=0)

    def block_over_samples(local):
        rows, width = local.shape
        cut = local.astype(jnp.bfloat16).reshape(rows, near, width // near)
        arrived = exchange(cut.transpose(1, 0, 2), "samp", level)
        part = jnp.sum(arrived.astype(jnp.float32), axis=0).astype(jnp.bfloat16)
        held = from_all(part, "samp", far, column)
        share = jnp.sum(held.astype(jnp.float32), axis=0).astype(jnp.bfloat16)
        whole = from_all(share, "samp", near, level)
        return whole.transpose(1, 0, 2).reshape(rows, width)

    def per_device(genotype, basis):
        samples, snps = genotype.shape
        total = samples * lax.axis_size("samp")
        observed = genotype < 3
        dosage = jnp.where(observed, genotype, 0)
        counts = jnp.stack([jnp.sum(dosage, axis=0), jnp.sum(observed.astype(jnp.int32), axis=0)])
        counts = over_samples(counts.reshape(-1, LANES)).reshape(2, snps).astype(jnp.float32)
        freq = (counts[0] + 1.0) / (2.0 * counts[1] + 2.0)
        scale = 1.0 / jnp.sqrt(2.0 * freq * (1.0 - freq))
        standard = jnp.where(
            observed, (dosage.astype(jnp.float32) - 2.0 * freq) * scale, 0.0
        ).astype(jnp.bfloat16)
        block = basis.T
        for step in range(ITERS):
            part = lax.dot_general(
                block, standard, (((1,), (1,)), ((), ())), preferred_element_type=jnp.float32
            ).astype(jnp.bfloat16)
            held = from_all(part, "snp", peers)
            scores = jnp.sum(held.astype(jnp.float32), axis=0).astype(jnp.bfloat16)
            local = jnp.dot(scores, standard, preferred_element_type=jnp.float32)
            snp_block = block_over_samples(local).astype(jnp.float32) / total
            block = snp_block.astype(jnp.bfloat16)
        return scores.T, snp_block.T

    return jax.shard_map(
        per_device,
        mesh=mesh,
        in_specs=(P("samp", "snp"), P("snp", None)),
        out_specs=(P("samp", None), P("snp", None)),
        check_vma=False,
    )
```

time: 157 us -> 138 us (0.88)
  blocking collectives: 149 us -> 131 us
  local copies, waits for them, and re-layouts: 2.51 us -> 0.27 us
    all_to_all x7 -> x10, blocking collectives: 149 us -> 131 us  [exchange(): lax.all_to_all(blocks, axis, split_axis=0, concat_axis=0, tiled=True, axi...]
    unnamed x15 -> x6, local copies, waits for them, and re-layouts: 1.93 us -> 0.02 us
where the time goes in v1:
time: 138 us; the launch traced here: 137 us
  blocking collectives  131 us (95%)
  other arithmetic  3.58 us (3%)
  matrix products  1.41 us (1%)
    all_to_all x10, blocking collectives, exchange(): lax.all_to_all(blocks, axis, split_axis=0, concat_axis=0, tiled=True, axi...  131 us

profile of v1, /device:TPU:1, one launch (start us, length us, event | category | flops | bytes accessed | tf_op | source)
XLA Modules:
  0.0 137.4 jit_solution(9897155883985660866)
XLA Ops:
  0.6 0.0 copy-start
  0.6 0.0 copy-start.1
  0.7 2.1 %select_reduce_fusion = (s32[512]{0:T(512)S(1)}, s32[512]{0:T(512)S(1)}) fusion(s32[1024,512]{1,0:T(8,128)} %param.2), kind=kLoop, calls=%fused_computation.2 | loop fusion | flops 2620416 | bytes 2101248 | tf_op jit(solution)/shard_map/reduce_sum | solution.py:55
  2.9 12.3 %all_to_all.50 = s16[4,8,128]{2,1,0:T(8,128)(2,1)S(1)} all-to-all(s16[4,8,128]{2,1,0:T(8,128)(2,1)S(1)} %broadcast_in_dim.35), channel_id=1, replica_groups={{0,8,256,264},{16,24,272,280},{32,40,288,296},{48,56,304,312},{64,72,32..., dimensions={0} | all-to-all | bytes 16384 | tf_op jit(solution)/shard_map/all_to_all | solution.py:20
  15.2 21.1 %all_to_all.51 = s16[16,8,128]{2,1,0:T(8,128)(2,1)S(1)} all-to-all(s16[16,8,128]{2,1,0:T(8,128)(2,1)S(1)} %broadcast_in_dim.36), channel_id=1, replica_groups={{0,16,32,48,64,80,96,112,128,144,160,176,192,208,224,240},{8,24,40,56,7..., dimensions={0} | all-to-all | bytes 65536 | tf_op jit(solution)/shard_map/all_to_all | solution.py:20
  36.4 0.0 copy-done.1
  36.4 0.5 select_convert_fusion
  36.9 0.0 copy-done
  36.9 0.4 fusion
  37.3 0.1 broadcast_in_dim.38
  37.4 16.2 %all_to_all.52 = bf16[8,40,1024]{2,1,0:T(8,128)(2,1)S(1)} all-to-all(bf16[8,40,1024]{2,1,0:T(8,128)(2,1)S(1)} %broadcast_in_dim.38), channel_id=1, replica_groups=mesh['samp'=64,'snp'=8] {'snp'}, dimensions={0} | all-to-all | bytes 1310720 | tf_op jit(solution)/shard_map/all_to_all | solution.py:20
  53.5 0.1 reduce_sum.112
  53.6 0.3 fusion.1
  54.0 9.3 %all_to_all.53 = bf16[4,40,128]{2,1,0:T(8,128)(2,1)S(1)} all-to-all(bf16[4,40,128]{2,1,0:T(8,128)(2,1)S(1)} %bitcast.47), channel_id=1, replica_groups={{0,8,256,264},{16,24,272,280},{32,40,288,296},{48,56,304,312},{64,72,32..., dimensions={0} | all-to-all | bytes 81920 | tf_op jit(solution)/shard_map/all_to_all | solution.py:20
  63.3 14.8 %all_to_all.54 = bf16[16,40,128]{2,1,0:T(8,128)(2,1)S(1)} all-to-all(bf16[16,40,128]{2,1,0:T(8,128)(2,1)S(1)} %broadcast_in_dim.39), channel_id=1, replica_groups={{0,16,32,48,64,80,96,112,128,144,160,176,192,208,224,240},{8,24,40,56,7..., dimensions={0} | all-to-all | bytes 327680 | tf_op jit(solution)/shard_map/all_to_all | solution.py:20
  78.2 9.6 %all_to_all.55 = bf16[4,40,128]{2,1,0:T(8,128)(2,1)S(1)} all-to-all(bf16[4,40,128]{2,1,0:T(8,128)(2,1)S(1)} %broadcast_in_dim.40), channel_id=1, replica_groups={{0,8,256,264},{16,24,272,280},{32,40,288,296},{48,56,304,312},{64,72,32..., dimensions={0} | all-to-all | bytes 81920 | tf_op jit(solution)/shard_map/all_to_all | solution.py:20
  87.8 0.4 convolution_convert_fusion
  88.2 0.1 broadcast_in_dim.41
  88.3 13.7 %all_to_all.56 = bf16[8,40,1024]{2,1,0:T(8,128)(2,1)S(1)} all-to-all(bf16[8,40,1024]{2,1,0:T(8,128)(2,1)S(1)} %broadcast_in_dim.41), channel_id=1, replica_groups=mesh['samp'=64,'snp'=8] {'snp'}, dimensions={0} | all-to-all | bytes 1310720 | tf_op jit(solution)/shard_map/all_to_all | solution.py:20
  101.9 0.1 reduce_sum.115
  102.0 0.0 copy-start.2
  102.1 0.3 fusion.2
  102.4 8.1 %all_to_all.57 = bf16[4,40,128]{2,1,0:T(8,128)(2,1)S(1)} all-to-all(bf16[4,40,128]{2,1,0:T(8,128)(2,1)S(1)} %bitcast.48), channel_id=1, replica_groups={{0,8,256,264},{16,24,272,280},{32,40,288,296},{48,56,304,312},{64,72,32..., dimensions={0} | all-to-all | bytes 81920 | tf_op jit(solution)/shard_map/all_to_all | solution.py:20
  110.5 16.3 %all_to_all.58 = bf16[16,40,128]{2,1,0:T(8,128)(2,1)S(1)} all-to-all(bf16[16,40,128]{2,1,0:T(8,128)(2,1)S(1)} %broadcast_in_dim.42), channel_id=1, replica_groups={{0,16,32,48,64,80,96,112,128,144,160,176,192,208,224,240},{8,24,40,56,7..., dimensions={0} | all-to-all | bytes 327680 | tf_op jit(solution)/shard_map/all_to_all | solution.py:20
  126.8 9.9 %all_to_all.59 = bf16[4,40,128]{2,1,0:T(8,128)(2,1)S(1)} all-to-all(bf16[4,40,128]{2,1,0:T(8,128)(2,1)S(1)} %broadcast_in_dim.43), channel_id=1, replica_groups={{0,8,256,264},{16,24,272,280},{32,40,288,296},{48,56,304,312},{64,72,32..., dimensions={0} | all-to-all | bytes 81920 | tf_op jit(solution)/shard_map/all_to_all | solution.py:20
  136.8 0.6 bitcast_bitcast_fusion
  137.4 0.0 copy-done.2
  (24 shorter events, 0.3 us)
Async XLA Ops:
  0.6 36.2 %copy-start = (bf16[512,40]{0,1:T(8,128)(2,1)S(1)}, bf16[512,40]{0,1:T(8,128)(2,1)}, u32[]{:S(2)}) copy-start(bf16[512,40]{0,1:T(8,128)(2,1)} %param.3) | copy-start | bytes 122884
  0.6 35.7 %copy-start.1 = (s32[1024,512]{1,0:T(8,128)S(1)}, s32[1024,512]{1,0:T(8,128)}, u32[]{:S(2)}) copy-start(s32[1024,512]{1,0:T(8,128)} %param.2) | copy-start | bytes 6291460
  102.0 35.4 %copy-start.2 = (bf16[40,1024]{1,0:T(8,128)(2,1)}, bf16[40,1024]{1,0:T(8,128)(2,1)S(1)}, u32[]{:S(2)}) copy-start(bf16[40,1024]{1,0:T(8,128)(2,1)S(1)} %reduce_sum.115) | copy-start | bytes 245764

commit v2 on v1

v2 whole, which is shorter than its diff:
```python
import jax
import jax.numpy as jnp
from jax import lax
from jax.sharding import PartitionSpec as P

ITERS = 2
LANES = 128
SUBLANES = 8
HALF = 16


def samp_groups(mesh):
    depth = mesh.shape["samp"] // 4
    at = lambda y, z, c: (y * depth + z) * 2 + c
    four = [(y, c) for y in range(2) for c in range(2)]
    level = [[at(y, z, c) for y, c in four] for z in range(depth)]
    column = [[at(y, z, c) for z in range(depth)] for y, c in four]
    cell = [[at(y, z + k, c) for k in range(2) for y, c in four] for z in range(0, depth, 2)]
    stride = [[at(y, z, c) for z in range(k, depth, 2)] for k in range(2) for y, c in four]
    return level, column, cell, stride


def exchange(blocks, axis, groups):
    return lax.all_to_all(
        blocks, axis, split_axis=0, concat_axis=0, tiled=True, axis_index_groups=groups
    )


def from_all(shard, axis, groups):
    copies = jnp.broadcast_to(shard, (len(groups[0]), *shard.shape))
    return exchange(copies, axis, groups)


def total_of(held):
    return jnp.sum(held.astype(jnp.float32), axis=0).astype(jnp.bfloat16)


def solution(mesh):
    level, column, cell, stride = samp_groups(mesh)
    peers = mesh.shape["snp"]
    snake = [[*range(0, peers, 2), *range(peers - 1, 0, -2)]]

    def block_over_samples(local):
        rows, width = local.shape
        members, tiles = len(cell[0]), width // LANES
        used = rows // SUBLANES * tiles
        each = -(-used // members)
        cut = local.astype(jnp.bfloat16).reshape(-1, SUBLANES, tiles, LANES)
        cut = cut.transpose(0, 2, 1, 3).reshape(used, SUBLANES, LANES)
        cut = jnp.pad(cut, ((0, each * members - used), (0, 0), (0, 0)))
        part = total_of(exchange(cut.reshape(members, each, SUBLANES, LANES), "samp", cell))
        share = total_of(from_all(part, "samp", stride))
        whole = from_all(share, "samp", cell).reshape(-1, SUBLANES, LANES)[:used]
        whole = whole.reshape(-1, tiles, SUBLANES, LANES).transpose(0, 2, 1, 3)
        return whole.reshape(rows, width)

    def per_device(genotype, basis):
        samples, snps = genotype.shape
        total = samples * lax.axis_size("samp")
        observed = genotype < 3
        counts = jnp.sum(jnp.where(observed, genotype + (1 << HALF), 0), axis=0)
        counts = jnp.sum(from_all(counts.reshape(-1, LANES), "samp", level), axis=0)
        held = from_all(counts, "samp", column)
        allele_sum = jnp.sum(held & ((1 << HALF) - 1), axis=0).astype(jnp.float32)
        called = jnp.sum(held >> HALF, axis=0).astype(jnp.float32)
        freq = (allele_sum + 1.0) / (2.0 * called + 2.0)
        scale = 1.0 / jnp.sqrt(2.0 * freq * (1.0 - freq))
        freq, scale = freq.reshape(snps), scale.reshape(snps)
        standard = jnp.where(
            observed, (genotype.astype(jnp.float32) - 2.0 * freq) * scale, 0.0
        ).astype(jnp.bfloat16)
        block = basis.T
        for step in range(ITERS):
            part = lax.dot_general(
                block, standard, (((1,), (1,)), ((), ())), preferred_element_type=jnp.float32
            ).astype(jnp.bfloat16)
            scores = total_of(from_all(part, "snp", snake))
            local = jnp.dot(scores, standard, preferred_element_type=jnp.float32)
            snp_block = block_over_samples(local).astype(jnp.float32) / total
            block = snp_block.astype(jnp.bfloat16)
        return scores.T, snp_block.T

    return jax.shard_map(
        per_device,
        mesh=mesh,
        in_specs=(P("samp", "snp"), P("snp", None)),
        out_specs=(P("samp", None), P("snp", None)),
        check_vma=False,
    )
```

time: 138 us -> 134 us (0.971)
  blocking collectives: 131 us -> 128 us
    all_to_all x10, blocking collectives: 131 us -> 128 us  [exchange(): lax.all_to_all(blocks, axis, split_axis=0, concat_axis=0, tiled=True, axi...]
where the time goes in v2:
time: 134 us
  blocking collectives  128 us (96%)
  other arithmetic  3.43 us (3%)
  matrix products  1.39 us (1%)
    all_to_all x10, blocking collectives, exchange(): lax.all_to_all(blocks, axis, split_axis=0, concat_axis=0, tiled=True, axi...  128 us

profile of v2, /device:TPU:1, one launch (start us, length us, event | category | flops | bytes accessed | tf_op | source)
XLA Modules:
  0.0 134.0 jit_solution(4292360186695820666)
XLA Ops:
  0.6 0.0 copy-start
  0.6 0.0 copy-start.1
  0.7 2.1 %select_reduce_fusion = s32[512]{0:T(512)S(1)} fusion(s32[1024,512]{1,0:T(8,128)} %param.2), kind=kLoop, calls=%fused_computation.1 | loop fusion | flops 2096640 | bytes 2099200 | tf_op jit(solution)/shard_map/reduce_sum | solution.py:61
  2.7 12.3 %all_to_all.50 = s32[4,4,128]{2,1,0:T(4,128)S(1)} all-to-all(s32[4,4,128]{2,1,0:T(4,128)S(1)} %broadcast_in_dim.34), channel_id=1, replica_groups={{0,8,256,264},{16,24,272,280},{32,40,288,296},{48,56,304,312},{64,72,32..., dimensions={0} | all-to-all | bytes 16384 | tf_op jit(solution)/shard_map/all_to_all | solution.py:24
  15.1 21.1 %all_to_all.51 = s32[16,4,128]{2,1,0:T(4,128)S(1)} all-to-all(s32[16,4,128]{2,1,0:T(4,128)S(1)} %broadcast_in_dim.35), channel_id=1, replica_groups={{0,16,32,48,64,80,96,112,128,144,160,176,192,208,224,240},{8,24,40,56,7..., dimensions={0} | all-to-all | bytes 65536 | tf_op jit(solution)/shard_map/all_to_all | solution.py:24
  36.2 0.0 copy-done.1
  36.3 0.4 select_convert_fusion
  36.7 0.0 copy-done
  36.7 0.4 fusion
  37.1 0.1 broadcast_in_dim.37
  37.2 16.1 %all_to_all.52 = bf16[8,40,1024]{2,1,0:T(8,128)(2,1)S(1)} all-to-all(bf16[8,40,1024]{2,1,0:T(8,128)(2,1)S(1)} %broadcast_in_dim.37), channel_id=1, replica_groups={{0,2,4,6,7,5,3,1},{8,10,12,14,15,13,11,9},{16,18,20,22,23,21,19,17},{24..., dimensions={0} | all-to-all | bytes 1310720 | tf_op jit(solution)/shard_map/all_to_all | solution.py:24
  53.3 0.1 reduce_sum.112
  53.4 0.3 convolution_convert_fusion.3
  53.7 10.3 %all_to_all.53 = bf16[8,3,8,128]{3,2,1,0:T(8,128)(2,1)S(1)} all-to-all(bf16[8,3,8,128]{3,2,1,0:T(8,128)(2,1)S(1)} %bitcast.47), channel_id=1, replica_groups={{0,8,256,264,16,24,272,280},{32,40,288,296,48,56,304,312},{64,72,320,32..., dimensions={0} | all-to-all | bytes 98304 | tf_op jit(solution)/shard_map/all_to_all | solution.py:24
  64.1 14.2 %all_to_all.54 = bf16[8,3,8,128]{3,2,1,0:T(8,128)(2,1)S(1)} all-to-all(bf16[8,3,8,128]{3,2,1,0:T(8,128)(2,1)S(1)} %broadcast_in_dim.38), channel_id=1, replica_groups={{0,32,64,96,128,160,192,224},{8,40,72,104,136,168,200,232},{256,288,320..., dimensions={0} | all-to-all | bytes 98304 | tf_op jit(solution)/shard_map/all_to_all | solution.py:24
  78.3 8.6 %all_to_all.55 = bf16[8,3,8,128]{3,2,1,0:T(8,128)(2,1)S(1)} all-to-all(bf16[8,3,8,128]{3,2,1,0:T(8,128)(2,1)S(1)} %broadcast_in_dim.39), channel_id=1, replica_groups={{0,8,256,264,16,24,272,280},{32,40,288,296,48,56,304,312},{64,72,320,32..., dimensions={0} | all-to-all | bytes 98304 | tf_op jit(solution)/shard_map/all_to_all | solution.py:24
  87.0 0.4 convolution_convert_fusion
  87.4 0.1 broadcast_in_dim.40
  87.5 13.8 %all_to_all.56 = bf16[8,40,1024]{2,1,0:T(8,128)(2,1)S(1)} all-to-all(bf16[8,40,1024]{2,1,0:T(8,128)(2,1)S(1)} %broadcast_in_dim.40), channel_id=1, replica_groups={{0,2,4,6,7,5,3,1},{8,10,12,14,15,13,11,9},{16,18,20,22,23,21,19,17},{24..., dimensions={0} | all-to-all | bytes 1310720 | tf_op jit(solution)/shard_map/all_to_all | solution.py:24
  101.2 0.1 reduce_sum.115
  101.3 0.0 copy-start.2
  101.3 0.3 convolution_convert_fusion.2
  101.6 8.9 %all_to_all.57 = bf16[8,3,8,128]{3,2,1,0:T(8,128)(2,1)S(1)} all-to-all(bf16[8,3,8,128]{3,2,1,0:T(8,128)(2,1)S(1)} %bitcast.48), channel_id=1, replica_groups={{0,8,256,264,16,24,272,280},{32,40,288,296,48,56,304,312},{64,72,320,32..., dimensions={0} | all-to-all | bytes 98304 | tf_op jit(solution)/shard_map/all_to_all | solution.py:24
  110.6 14.4 %all_to_all.58 = bf16[8,3,8,128]{3,2,1,0:T(8,128)(2,1)S(1)} all-to-all(bf16[8,3,8,128]{3,2,1,0:T(8,128)(2,1)S(1)} %broadcast_in_dim.41), channel_id=1, replica_groups={{0,32,64,96,128,160,192,224},{8,40,72,104,136,168,200,232},{256,288,320..., dimensions={0} | all-to-all | bytes 98304 | tf_op jit(solution)/shard_map/all_to_all | solution.py:24
  125.1 8.3 %all_to_all.59 = bf16[8,3,8,128]{3,2,1,0:T(8,128)(2,1)S(1)} all-to-all(bf16[8,3,8,128]{3,2,1,0:T(8,128)(2,1)S(1)} %broadcast_in_dim.42), channel_id=1, replica_groups={{0,8,256,264,16,24,272,280},{32,40,288,296,48,56,304,312},{64,72,320,32..., dimensions={0} | all-to-all | bytes 98304 | tf_op jit(solution)/shard_map/all_to_all | solution.py:24
  133.3 0.6 convert_multiply_fusion
  134.0 0.0 copy-done.2
  (17 shorter events, 0.2 us)
Async XLA Ops:
  0.6 36.0 %copy-start = (bf16[512,40]{0,1:T(8,128)(2,1)S(1)}, bf16[512,40]{0,1:T(8,128)(2,1)}, u32[]{:S(2)}) copy-start(bf16[512,40]{0,1:T(8,128)(2,1)} %param.3) | copy-start | bytes 122884
  0.6 35.6 %copy-start.1 = (s32[1024,512]{1,0:T(8,128)S(1)}, s32[1024,512]{1,0:T(8,128)}, u32[]{:S(2)}) copy-start(s32[1024,512]{1,0:T(8,128)} %param.2) | copy-start | bytes 6291460
  101.3 32.6 %copy-start.2 = (bf16[40,1024]{1,0:T(8,128)(2,1)}, bf16[40,1024]{1,0:T(8,128)(2,1)S(1)}, u32[]{:S(2)}) copy-start(bf16[40,1024]{1,0:T(8,128)(2,1)S(1)} %reduce_sum.115) | copy-start | bytes 245764

commit v3 on v2

v3 whole, which is shorter than its diff:
```python
import jax
import jax.numpy as jnp
from jax import lax
from jax.sharding import PartitionSpec as P

ITERS = 2
LANES = 128
SUBLANES = 8
HALF = 16


def samp_groups(mesh):
    depth = mesh.shape["samp"] // 4
    at = lambda y, z, c: (y * depth + z) * 2 + c
    four = [(y, c) for y in range(2) for c in range(2)]
    zigzag = [k // 2 if k % 2 == 0 else depth - 1 - k // 2 for k in range(depth)]
    chip = [[at(y, z, c) for c in range(2)] for z in range(depth) for y in range(2)]
    side = [[at(y, z, c) for y in range(2)] for z in range(depth) for c in range(2)]
    level = [[at(y, z, c) for y, c in four] for z in range(depth)]
    column = [[at(y, z, c) for z in zigzag] for y, c in four]
    return chip, side, level, column


def exchange(blocks, axis, groups):
    return lax.all_to_all(
        blocks, axis, split_axis=0, concat_axis=0, tiled=True, axis_index_groups=groups
    )


def from_all(shard, axis, groups):
    copies = jnp.broadcast_to(shard, (len(groups[0]), *shard.shape))
    return exchange(copies, axis, groups)


def gather(shard, axis, groups):
    return lax.all_gather(shard, axis, axis_index_groups=groups)


def total_of(held):
    return jnp.sum(held.astype(jnp.float32), axis=0).astype(jnp.bfloat16)


def solution(mesh):
    chip, side, level, column = samp_groups(mesh)
    peers = mesh.shape["snp"]
    snake = [[*range(0, peers, 2), *range(peers - 1, 0, -2)]]

    def block_over_samples(local, y, core):
        rows, width = local.shape
        tiles = width // LANES
        cut = local.astype(jnp.bfloat16).reshape(-1, SUBLANES, tiles, LANES).transpose(0, 2, 1, 3)
        cut = cut.reshape(2, 2, -1, SUBLANES, LANES)
        half = total_of(lax.dynamic_index_in_dim(gather(cut, "samp", chip), core, 2, False))
        part = total_of(lax.dynamic_index_in_dim(gather(half, "samp", side), y, 1, False))
        share = total_of(from_all(part, "samp", column))
        whole = gather(share, "samp", level)
        whole = whole.reshape(-1, tiles, SUBLANES, LANES).transpose(0, 2, 1, 3)
        return whole.reshape(rows, width)

    def per_device(genotype, basis):
        samples, snps = genotype.shape
        total = samples * lax.axis_size("samp")
        at = lax.axis_index("samp").astype(jnp.uint32)
        y, core = (at >= lax.axis_size("samp") // 2).astype(jnp.uint32), at & 1
        observed = genotype < 3
        counts = jnp.sum(jnp.where(observed, genotype + (1 << HALF), 0), axis=0)
        counts, y, core = lax.optimization_barrier((counts, y, core))
        counts = jnp.sum(gather(counts.reshape(-1, LANES), "samp", level), axis=0)
        held = from_all(counts, "samp", column)
        allele_sum = jnp.sum(held & ((1 << HALF) - 1), axis=0).astype(jnp.float32)
        called = jnp.sum(held >> HALF, axis=0).astype(jnp.float32)
        freq = (allele_sum + 1.0) / (2.0 * called + 2.0)
        scale = 1.0 / jnp.sqrt(2.0 * freq * (1.0 - freq))
        freq, scale = freq.reshape(snps), scale.reshape(snps)
        standard = jnp.where(
            observed, (genotype.astype(jnp.float32) - 2.0 * freq) * scale, 0.0
        ).astype(jnp.bfloat16)
        block = basis.T
        for step in range(ITERS):
            part = lax.dot_general(
                block, standard, (((1,), (1,)), ((), ())), preferred_element_type=jnp.float32
            ).astype(jnp.bfloat16)
            scores = total_of(from_all(part, "snp", snake))
            local = jnp.dot(scores, standard, preferred_element_type=jnp.float32)
            snp_block = block_over_samples(local, y, core).astype(jnp.float32) / total
            block = snp_block.astype(jnp.bfloat16)
        return scores.T, snp_block.T

    return jax.shard_map(
        per_device,
        mesh=mesh,
        in_specs=(P("samp", "snp"), P("snp", None)),
        out_specs=(P("samp", None), P("snp", None)),
        check_vma=False,
    )
```

time: 134 us -> 137 us (1.022)
  blocking collectives: 128 us -> 131 us
    all_gather x0 -> x7, blocking collectives: none -> 44 us  [gather(): return lax.all_gather(shard, axis, axis_index_groups=groups)]
    all_to_all x10 -> x5, blocking collectives: 128 us -> 87.1 us  [exchange(): lax.all_to_all(blocks, axis, split_axis=0, concat_axis=0, tiled=True, axi...]
where the time goes in v3:
time: 137 us
  blocking collectives  131 us (96%)
  other arithmetic  3.47 us (3%)
  matrix products  1.38 us (1%)
    all_to_all x5, blocking collectives, exchange(): lax.all_to_all(blocks, axis, split_axis=0, concat_axis=0, tiled=True, axi...  87.1 us
    all_gather x7, blocking collectives, gather(): return lax.all_gather(shard, axis, axis_index_groups=groups)  44 us

profile of v3, /device:TPU:1, one launch (start us, length us, event | category | flops | bytes accessed | tf_op | source)
XLA Modules:
  0.0 136.9 jit_solution(11561856409951315793)
XLA Ops:
  0.6 0.0 copy-start
  0.6 0.0 copy-start.1
  0.7 2.1 %select_reduce_fusion = s32[512]{0:T(512)S(1)} fusion(s32[1024,512]{1,0:T(8,128)} %param.2), kind=kLoop, calls=%fused_computation.1 | loop fusion | flops 2096640 | bytes 2099200 | tf_op jit(solution)/shard_map/reduce_sum | solution.py:66
  2.7 11.8 %all_gather.33 = s32[4,4,128]{2,1,0:T(4,128)S(1)} all-gather(s32[1,4,128]{2,1,0:T(4,128)S(1)} %bitcast.51), channel_id=1, replica_groups={{0,8,256,264},{16,24,272,280},{32,40,288,296},{48,56,304,312},{64,72,32..., dimensions={0}, use_global_device_ids=true | all-gather | bytes 10240 | tf_op jit(solution)/shard_map/all_gather | solution.py:36
  14.6 21.2 %all_to_all.25 = s32[16,4,128]{2,1,0:T(4,128)S(1)} all-to-all(s32[16,4,128]{2,1,0:T(4,128)S(1)} %broadcast_in_dim.25), channel_id=1, replica_groups={{0,240,16,224,32,208,48,192,64,176,80,160,96,144,112,128},{8,248,24,232..., dimensions={0} | all-to-all | bytes 65536 | tf_op jit(solution)/shard_map/all_to_all | solution.py:25
  35.8 0.0 copy-done.1
  35.8 0.4 select_convert_fusion
  36.2 0.0 copy-done
  36.2 0.4 fusion
  36.6 0.1 broadcast_in_dim.27
  36.7 17.1 %all_to_all.26 = bf16[8,40,1024]{2,1,0:T(8,128)(2,1)S(1)} all-to-all(bf16[8,40,1024]{2,1,0:T(8,128)(2,1)S(1)} %broadcast_in_dim.27), channel_id=1, replica_groups={{0,2,4,6,7,5,3,1},{8,10,12,14,15,13,11,9},{16,18,20,22,23,21,19,17},{24..., dimensions={0} | all-to-all | bytes 1310720 | tf_op jit(solution)/shard_map/all_to_all | solution.py:25
  53.8 0.1 reduce_sum.136
  53.9 0.3 convolution_convert_fusion.3
  54.2 4.8 %all_gather.34 = bf16[2,2,2,5,8,128]{5,4,3,2,1,0:T(8,128)(2,1)S(1)} all-gather(bf16[1,2,2,5,8,128]{5,4,3,2,1,0:T(8,128)(2,1)S(1)} %bitcast.46), channel_id=1, replica_groups={{0,8},{256,264},{16,24},{272,280},{32,40},{288,296},{48,56},{304,312},{..., dimensions={0}, use_global_device_ids=true | all-gather | bytes 122880 | tf_op jit(solution)/shard_map/all_gather | solution.py:36
  59.0 3.3 %all-gather = bf16[4,5,8,128]{3,2,1,0:T(8,128)(2,1)S(1)} all-gather(bf16[2,5,8,128]{3,2,1,0:T(8,128)(2,1)S(1)} %dynamic-slice_reduce_fusion.1), channel_id=2, replica_groups={{0,256},{8,264},{16,272},{24,280},{32,288},{40,296},{48,304},{56,312},{..., dimensions={0}, use_global_device_ids=true | all-gather | bytes 61440 | tf_op jit(solution)/shard_map/all_gather | solution.py:36
  62.3 17.2 %all_to_all.27 = bf16[16,5,8,128]{3,2,1,0:T(8,128)(2,1)S(1)} all-to-all(bf16[16,5,8,128]{3,2,1,0:T(8,128)(2,1)S(1)} %broadcast_in_dim.28), channel_id=1, replica_groups={{0,240,16,224,32,208,48,192,64,176,80,160,96,144,112,128},{8,248,24,232..., dimensions={0} | all-to-all | bytes 327680 | tf_op jit(solution)/shard_map/all_to_all | solution.py:25
  79.5 8.8 %all-gather.1 = bf16[20,8,128]{2,1,0:T(8,128)(2,1)S(1)} all-gather(bf16[5,8,128]{2,1,0:T(8,128)(2,1)S(1)} %reduce_sum.139), channel_id=3, replica_groups={{0,8,256,264},{16,24,272,280},{32,40,288,296},{48,56,304,312},{64,72,32..., dimensions={0}, use_global_device_ids=true | all-gather | bytes 51200 | tf_op jit(solution)/shard_map/all_gather | solution.py:36
  88.3 0.4 convolution_convert_fusion
  88.7 0.1 broadcast_in_dim.29
  88.8 14.6 %all_to_all.28 = bf16[8,40,1024]{2,1,0:T(8,128)(2,1)S(1)} all-to-all(bf16[8,40,1024]{2,1,0:T(8,128)(2,1)S(1)} %broadcast_in_dim.29), channel_id=1, replica_groups={{0,2,4,6,7,5,3,1},{8,10,12,14,15,13,11,9},{16,18,20,22,23,21,19,17},{24..., dimensions={0} | all-to-all | bytes 1310720 | tf_op jit(solution)/shard_map/all_to_all | solution.py:25
  103.4 0.1 reduce_sum.140
  103.5 0.0 copy-start.2
  103.5 0.3 convolution_convert_fusion.2
  103.8 3.2 %all_gather.39 = bf16[2,2,2,5,8,128]{5,4,3,2,1,0:T(8,128)(2,1)S(1)} all-gather(bf16[1,2,2,5,8,128]{5,4,3,2,1,0:T(8,128)(2,1)S(1)} %bitcast.47), channel_id=1, replica_groups={{0,8},{256,264},{16,24},{272,280},{32,40},{288,296},{48,56},{304,312},{..., dimensions={0}, use_global_device_ids=true | all-gather | bytes 122880 | tf_op jit(solution)/shard_map/all_gather | solution.py:36
  107.0 3.3 %all-gather.2 = bf16[4,5,8,128]{3,2,1,0:T(8,128)(2,1)S(1)} all-gather(bf16[2,5,8,128]{3,2,1,0:T(8,128)(2,1)S(1)} %dynamic-slice_reduce_fusion), channel_id=4, replica_groups={{0,256},{8,264},{16,272},{24,280},{32,288},{40,296},{48,304},{56,312},{..., dimensions={0}, use_global_device_ids=true | all-gather | bytes 61440 | tf_op jit(solution)/shard_map/all_gather | solution.py:36
  110.3 17.2 %all_to_all.29 = bf16[16,5,8,128]{3,2,1,0:T(8,128)(2,1)S(1)} all-to-all(bf16[16,5,8,128]{3,2,1,0:T(8,128)(2,1)S(1)} %broadcast_in_dim.30), channel_id=1, replica_groups={{0,240,16,224,32,208,48,192,64,176,80,160,96,144,112,128},{8,248,24,232..., dimensions={0} | all-to-all | bytes 327680 | tf_op jit(solution)/shard_map/all_to_all | solution.py:25
  127.5 8.8 %all-gather.3 = bf16[20,8,128]{2,1,0:T(8,128)(2,1)S(1)} all-gather(bf16[5,8,128]{2,1,0:T(8,128)(2,1)S(1)} %reduce_sum.143), channel_id=5, replica_groups={{0,8,256,264},{16,24,272,280},{32,40,288,296},{48,56,304,312},{64,72,32..., dimensions={0}, use_global_device_ids=true | all-gather | bytes 51200 | tf_op jit(solution)/shard_map/all_gather | solution.py:36
  136.3 0.6 convert_multiply_fusion
  136.9 0.0 copy-done.2
  (14 shorter events, 0.2 us)
Async XLA Ops:
  0.6 35.6 %copy-start = (bf16[512,40]{0,1:T(8,128)(2,1)S(1)}, bf16[512,40]{0,1:T(8,128)(2,1)}, u32[]{:S(2)}) copy-start(bf16[512,40]{0,1:T(8,128)(2,1)} %param.3) | copy-start | bytes 122884
  0.6 35.1 %copy-start.1 = (s32[1024,512]{1,0:T(8,128)S(1)}, s32[1024,512]{1,0:T(8,128)}, u32[]{:S(2)}) copy-start(s32[1024,512]{1,0:T(8,128)} %param.2) | copy-start | bytes 6291460
  103.5 33.5 %copy-start.2 = (bf16[40,1024]{1,0:T(8,128)(2,1)}, bf16[40,1024]{1,0:T(8,128)(2,1)S(1)}, u32[]{:S(2)}) copy-start(bf16[40,1024]{1,0:T(8,128)(2,1)S(1)} %reduce_sum.140) | copy-start | bytes 245764

commit v4 on v2

--- a/solution.py
+++ b/solution.py
@@ -32,7 +32,7 @@
 
 
 def total_of(held):
-    return jnp.sum(held.astype(jnp.float32), axis=0).astype(jnp.bfloat16)
+    return jnp.sum(held.astype(jnp.float32), axis=0)
 
 
 def solution(mesh):
@@ -40,19 +40,15 @@
     peers = mesh.shape["snp"]
     snake = [[*range(0, peers, 2), *range(peers - 1, 0, -2)]]
 
-    def block_over_samples(local):
+    def block_over_samples(local, total, dtype):
         rows, width = local.shape
         members, tiles = len(cell[0]), width // LANES
-        used = rows // SUBLANES * tiles
-        each = -(-used // members)
         cut = local.astype(jnp.bfloat16).reshape(-1, SUBLANES, tiles, LANES)
-        cut = cut.transpose(0, 2, 1, 3).reshape(used, SUBLANES, LANES)
-        cut = jnp.pad(cut, ((0, each * members - used), (0, 0), (0, 0)))
-        part = total_of(exchange(cut.reshape(members, each, SUBLANES, LANES), "samp", cell))
-        share = total_of(from_all(part, "samp", stride))
-        whole = from_all(share, "samp", cell).reshape(-1, SUBLANES, LANES)[:used]
-        whole = whole.reshape(-1, tiles, SUBLANES, LANES).transpose(0, 2, 1, 3)
-        return whole.reshape(rows, width)
+        cut = cut.transpose(0, 2, 1, 3).reshape(members, -1, SUBLANES // 2, LANES)
+        part = total_of(exchange(cut, "samp", cell)).astype(jnp.bfloat16)
+        share = (total_of(from_all(part, "samp", stride)) / total).astype(dtype)
+        whole = from_all(share, "samp", cell).reshape(-1, tiles, SUBLANES, LANES)
+        return whole.transpose(0, 2, 1, 3).reshape(rows, width)
 
     def per_device(genotype, basis):
         samples, snps = genotype.shape
@@ -74,11 +70,11 @@
             part = lax.dot_general(
                 block, standard, (((1,), (1,)), ((), ())), preferred_element_type=jnp.float32
             ).astype(jnp.bfloat16)
-            scores = total_of(from_all(part, "snp", snake))
+            scores = total_of(from_all(part, "snp", snake)).astype(jnp.bfloat16)
             local = jnp.dot(scores, standard, preferred_element_type=jnp.float32)
-            snp_block = block_over_samples(local).astype(jnp.float32) / total
-            block = snp_block.astype(jnp.bfloat16)
-        return scores.T, snp_block.T
+            last = step == ITERS - 1
+            block = block_over_samples(local, total, jnp.float32 if last else jnp.bfloat16)
+        return scores.T, block.T
 
     return jax.shard_map(
         per_device,

time: 134 us -> 134 us (level)
  no operation moved by 1% of the time
where the time goes in v4:
time: 134 us
  blocking collectives  128 us (96%)
  other arithmetic  2.88 us (2%)
  matrix products  1.38 us (1%)
    all_to_all x10, blocking collectives, exchange(): lax.all_to_all(blocks, axis, split_axis=0, concat_axis=0, tiled=True, axi...  128 us

profile of v4, /device:TPU:1, one launch (start us, length us, event | category | flops | bytes accessed | tf_op | source)
XLA Modules:
  0.0 133.8 jit_solution(645638352562173975)
XLA Ops:
  0.6 0.0 copy-start
  0.6 0.0 copy-start.1
  0.7 2.1 %select_reduce_fusion = s32[512]{0:T(512)S(1)} fusion(s32[1024,512]{1,0:T(8,128)} %param.2), kind=kLoop, calls=%fused_computation.1 | loop fusion | flops 2096640 | bytes 2099200 | tf_op jit(solution)/shard_map/reduce_sum | solution.py:57
  2.7 12.3 %all_to_all.50 = s32[4,4,128]{2,1,0:T(4,128)S(1)} all-to-all(s32[4,4,128]{2,1,0:T(4,128)S(1)} %broadcast_in_dim.34), channel_id=1, replica_groups={{0,8,256,264},{16,24,272,280},{32,40,288,296},{48,56,304,312},{64,72,32..., dimensions={0} | all-to-all | bytes 16384 | tf_op jit(solution)/shard_map/all_to_all | solution.py:24
  15.1 21.1 %all_to_all.51 = s32[16,4,128]{2,1,0:T(4,128)S(1)} all-to-all(s32[16,4,128]{2,1,0:T(4,128)S(1)} %broadcast_in_dim.35), channel_id=1, replica_groups={{0,16,32,48,64,80,96,112,128,144,160,176,192,208,224,240},{8,24,40,56,7..., dimensions={0} | all-to-all | bytes 65536 | tf_op jit(solution)/shard_map/all_to_all | solution.py:24
  36.2 0.0 copy-done.1
  36.3 0.4 select_convert_fusion
  36.7 0.0 copy-done
  36.7 0.4 fusion
  37.1 0.1 broadcast_in_dim.37
  37.2 16.1 %all_to_all.52 = bf16[8,40,1024]{2,1,0:T(8,128)(2,1)S(1)} all-to-all(bf16[8,40,1024]{2,1,0:T(8,128)(2,1)S(1)} %broadcast_in_dim.37), channel_id=1, replica_groups={{0,2,4,6,7,5,3,1},{8,10,12,14,15,13,11,9},{16,18,20,22,23,21,19,17},{24..., dimensions={0} | all-to-all | bytes 1310720 | tf_op jit(solution)/shard_map/all_to_all | solution.py:24
  53.3 0.1 reduce_sum.106
  53.4 0.3 convolution_convert_fusion.3
  53.7 10.3 %all_to_all.53 = bf16[8,5,4,128]{3,2,1,0:T(4,128)(2,1)S(1)} all-to-all(bf16[8,5,4,128]{3,2,1,0:T(4,128)(2,1)S(1)} %bitcast.44), channel_id=1, replica_groups={{0,8,256,264,16,24,272,280},{32,40,288,296,48,56,304,312},{64,72,320,32..., dimensions={0} | all-to-all | bytes 81920 | tf_op jit(solution)/shard_map/all_to_all | solution.py:24
  64.1 14.3 %all_to_all.54 = bf16[8,5,4,128]{3,2,1,0:T(4,128)(2,1)S(1)} all-to-all(bf16[8,5,4,128]{3,2,1,0:T(4,128)(2,1)S(1)} %broadcast_in_dim.38), channel_id=1, replica_groups={{0,32,64,96,128,160,192,224},{8,40,72,104,136,168,200,232},{256,288,320..., dimensions={0} | all-to-all | bytes 81920 | tf_op jit(solution)/shard_map/all_to_all | solution.py:24
  78.4 8.5 %all_to_all.55 = bf16[8,5,4,128]{3,2,1,0:T(4,128)(2,1)S(1)} all-to-all(bf16[8,5,4,128]{3,2,1,0:T(4,128)(2,1)S(1)} %broadcast_in_dim.39), channel_id=1, replica_groups={{0,8,256,264,16,24,272,280},{32,40,288,296,48,56,304,312},{64,72,320,32..., dimensions={0} | all-to-all | bytes 81920 | tf_op jit(solution)/shard_map/all_to_all | solution.py:24
  86.8 0.4 convolution_convert_fusion
  87.3 0.1 broadcast_in_dim.40
  87.3 13.8 %all_to_all.56 = bf16[8,40,1024]{2,1,0:T(8,128)(2,1)S(1)} all-to-all(bf16[8,40,1024]{2,1,0:T(8,128)(2,1)S(1)} %broadcast_in_dim.40), channel_id=1, replica_groups={{0,2,4,6,7,5,3,1},{8,10,12,14,15,13,11,9},{16,18,20,22,23,21,19,17},{24..., dimensions={0} | all-to-all | bytes 1310720 | tf_op jit(solution)/shard_map/all_to_all | solution.py:24
  101.1 0.1 reduce_sum.109
  101.2 0.0 copy-start.2
  101.2 0.3 convolution_convert_fusion.2
  101.5 8.9 %all_to_all.57 = bf16[8,5,4,128]{3,2,1,0:T(4,128)(2,1)S(1)} all-to-all(bf16[8,5,4,128]{3,2,1,0:T(4,128)(2,1)S(1)} %bitcast.46), channel_id=1, replica_groups={{0,8,256,264,16,24,272,280},{32,40,288,296,48,56,304,312},{64,72,320,32..., dimensions={0} | all-to-all | bytes 81920 | tf_op jit(solution)/shard_map/all_to_all | solution.py:24
  110.5 14.6 %all_to_all.58 = bf16[8,5,4,128]{3,2,1,0:T(4,128)(2,1)S(1)} all-to-all(bf16[8,5,4,128]{3,2,1,0:T(4,128)(2,1)S(1)} %broadcast_in_dim.41), channel_id=1, replica_groups={{0,32,64,96,128,160,192,224},{8,40,72,104,136,168,200,232},{256,288,320..., dimensions={0} | all-to-all | bytes 81920 | tf_op jit(solution)/shard_map/all_to_all | solution.py:24
  125.1 8.0 %all_to_all.59 = f32[8,5,4,128]{3,2,1,0:T(4,128)S(1)} all-to-all(f32[8,5,4,128]{3,2,1,0:T(4,128)S(1)} %broadcast_in_dim.42), channel_id=1, replica_groups={{0,8,256,264,16,24,272,280},{32,40,288,296,48,56,304,312},{64,72,320,32..., dimensions={0} | all-to-all | bytes 163840 | tf_op jit(solution)/shard_map/all_to_all | solution.py:24
  133.2 0.6 copy.18
  133.8 0.0 copy-done.2
  (16 shorter events, 0.3 us)
Async XLA Ops:
  0.6 36.0 %copy-start = (bf16[512,40]{0,1:T(8,128)(2,1)S(1)}, bf16[512,40]{0,1:T(8,128)(2,1)}, u32[]{:S(2)}) copy-start(bf16[512,40]{0,1:T(8,128)(2,1)} %param.3) | copy-start | bytes 122884
  0.6 35.6 %copy-start.1 = (s32[1024,512]{1,0:T(8,128)S(1)}, s32[1024,512]{1,0:T(8,128)}, u32[]{:S(2)}) copy-start(s32[1024,512]{1,0:T(8,128)} %param.2) | copy-start | bytes 6291460
  101.2 32.6 %copy-start.2 = (bf16[40,1024]{1,0:T(8,128)(2,1)}, bf16[40,1024]{1,0:T(8,128)(2,1)S(1)}, u32[]{:S(2)}) copy-start(bf16[40,1024]{1,0:T(8,128)(2,1)S(1)} %reduce_sum.109) | copy-start | bytes 245764

commit v5 on v4

--- a/solution.py
+++ b/solution.py
@@ -15,8 +15,9 @@
     four = [(y, c) for y in range(2) for c in range(2)]
     level = [[at(y, z, c) for y, c in four] for z in range(depth)]
     column = [[at(y, z, c) for z in range(depth)] for y, c in four]
-    cell = [[at(y, z + k, c) for k in range(2) for y, c in four] for z in range(0, depth, 2)]
-    stride = [[at(y, z, c) for z in range(k, depth, 2)] for k in range(2) for y, c in four]
+    twos = [(z, z + 1) if z < depth // 2 else (z + 1, z) for z in range(0, depth, 2)]
+    cell = [[at(y, z, c) for z in two for y, c in four] for two in twos]
+    stride = [[at(y, two[k], c) for two in twos] for k in range(2) for y, c in four]
     return level, column, cell, stride
 
 

time: 134 us -> 133 us (level)
  blocking collectives: 128 us -> 126 us
    all_to_all x10, blocking collectives: 128 us -> 126 us  [exchange(): lax.all_to_all(blocks, axis, split_axis=0, concat_axis=0, tiled=True, axi...]
where the time goes in v5:
time: 133 us; the launch traced here: 132 us
  blocking collectives  126 us (95%)
  other arithmetic  2.88 us (2%)
  matrix products  1.38 us (1%)
    all_to_all x10, blocking collectives, exchange(): lax.all_to_all(blocks, axis, split_axis=0, concat_axis=0, tiled=True, axi...  126 us

profile of v5, /device:TPU:1, one launch (start us, length us, event | category | flops | bytes accessed | tf_op | source)
XLA Modules:
  0.0 132.4 jit_solution(14416532514835071511)
XLA Ops:
  0.6 0.0 copy-start
  0.6 0.0 copy-start.1
  0.7 2.1 %select_reduce_fusion = s32[512]{0:T(512)S(1)} fusion(s32[1024,512]{1,0:T(8,128)} %param.2), kind=kLoop, calls=%fused_computation.1 | loop fusion | flops 2096640 | bytes 2099200 | tf_op jit(solution)/shard_map/reduce_sum | solution.py:58
  2.7 12.3 %all_to_all.50 = s32[4,4,128]{2,1,0:T(4,128)S(1)} all-to-all(s32[4,4,128]{2,1,0:T(4,128)S(1)} %broadcast_in_dim.34), channel_id=1, replica_groups={{0,8,256,264},{16,24,272,280},{32,40,288,296},{48,56,304,312},{64,72,32..., dimensions={0} | all-to-all | bytes 16384 | tf_op jit(solution)/shard_map/all_to_all | solution.py:25
  15.1 21.1 %all_to_all.51 = s32[16,4,128]{2,1,0:T(4,128)S(1)} all-to-all(s32[16,4,128]{2,1,0:T(4,128)S(1)} %broadcast_in_dim.35), channel_id=1, replica_groups={{0,16,32,48,64,80,96,112,128,144,160,176,192,208,224,240},{8,24,40,56,7..., dimensions={0} | all-to-all | bytes 65536 | tf_op jit(solution)/shard_map/all_to_all | solution.py:25
  36.2 0.0 copy-done.1
  36.3 0.4 select_convert_fusion
  36.7 0.0 copy-done
  36.7 0.4 fusion
  37.1 0.1 broadcast_in_dim.37
  37.2 16.1 %all_to_all.52 = bf16[8,40,1024]{2,1,0:T(8,128)(2,1)S(1)} all-to-all(bf16[8,40,1024]{2,1,0:T(8,128)(2,1)S(1)} %broadcast_in_dim.37), channel_id=1, replica_groups={{0,2,4,6,7,5,3,1},{8,10,12,14,15,13,11,9},{16,18,20,22,23,21,19,17},{24..., dimensions={0} | all-to-all | bytes 1310720 | tf_op jit(solution)/shard_map/all_to_all | solution.py:25
  53.3 0.1 reduce_sum.106
  53.4 0.3 convolution_convert_fusion.3
  53.7 10.3 %all_to_all.53 = bf16[8,5,4,128]{3,2,1,0:T(4,128)(2,1)S(1)} all-to-all(bf16[8,5,4,128]{3,2,1,0:T(4,128)(2,1)S(1)} %bitcast.44), channel_id=1, replica_groups={{0,8,256,264,16,24,272,280},{32,40,288,296,48,56,304,312},{64,72,320,32..., dimensions={0} | all-to-all | bytes 81920 | tf_op jit(solution)/shard_map/all_to_all | solution.py:25
  64.1 13.0 %all_to_all.54 = bf16[8,5,4,128]{3,2,1,0:T(4,128)(2,1)S(1)} all-to-all(bf16[8,5,4,128]{3,2,1,0:T(4,128)(2,1)S(1)} %broadcast_in_dim.38), channel_id=1, replica_groups={{0,32,64,96,144,176,208,240},{8,40,72,104,152,184,216,248},{256,288,320..., dimensions={0} | all-to-all | bytes 81920 | tf_op jit(solution)/shard_map/all_to_all | solution.py:25
  77.2 9.0 %all_to_all.55 = bf16[8,5,4,128]{3,2,1,0:T(4,128)(2,1)S(1)} all-to-all(bf16[8,5,4,128]{3,2,1,0:T(4,128)(2,1)S(1)} %broadcast_in_dim.39), channel_id=1, replica_groups={{0,8,256,264,16,24,272,280},{32,40,288,296,48,56,304,312},{64,72,320,32..., dimensions={0} | all-to-all | bytes 81920 | tf_op jit(solution)/shard_map/all_to_all | solution.py:25
  86.2 0.4 convolution_convert_fusion
  86.6 0.1 broadcast_in_dim.40
  86.7 13.8 %all_to_all.56 = bf16[8,40,1024]{2,1,0:T(8,128)(2,1)S(1)} all-to-all(bf16[8,40,1024]{2,1,0:T(8,128)(2,1)S(1)} %broadcast_in_dim.40), channel_id=1, replica_groups={{0,2,4,6,7,5,3,1},{8,10,12,14,15,13,11,9},{16,18,20,22,23,21,19,17},{24..., dimensions={0} | all-to-all | bytes 1310720 | tf_op jit(solution)/shard_map/all_to_all | solution.py:25
  100.5 0.1 reduce_sum.109
  100.6 0.0 copy-start.2
  100.6 0.3 convolution_convert_fusion.2
  100.9 8.9 %all_to_all.57 = bf16[8,5,4,128]{3,2,1,0:T(4,128)(2,1)S(1)} all-to-all(bf16[8,5,4,128]{3,2,1,0:T(4,128)(2,1)S(1)} %bitcast.46), channel_id=1, replica_groups={{0,8,256,264,16,24,272,280},{32,40,288,296,48,56,304,312},{64,72,320,32..., dimensions={0} | all-to-all | bytes 81920 | tf_op jit(solution)/shard_map/all_to_all | solution.py:25
  109.8 13.0 %all_to_all.58 = bf16[8,5,4,128]{3,2,1,0:T(4,128)(2,1)S(1)} all-to-all(bf16[8,5,4,128]{3,2,1,0:T(4,128)(2,1)S(1)} %broadcast_in_dim.41), channel_id=1, replica_groups={{0,32,64,96,144,176,208,240},{8,40,72,104,152,184,216,248},{256,288,320..., dimensions={0} | all-to-all | bytes 81920 | tf_op jit(solution)/shard_map/all_to_all | solution.py:25
  122.9 8.8 %all_to_all.59 = f32[8,5,4,128]{3,2,1,0:T(4,128)S(1)} all-to-all(f32[8,5,4,128]{3,2,1,0:T(4,128)S(1)} %broadcast_in_dim.42), channel_id=1, replica_groups={{0,8,256,264,16,24,272,280},{32,40,288,296,48,56,304,312},{64,72,320,32..., dimensions={0} | all-to-all | bytes 163840 | tf_op jit(solution)/shard_map/all_to_all | solution.py:25
  131.7 0.6 copy.18
  132.4 0.0 copy-done.2
  (16 shorter events, 0.3 us)
Async XLA Ops:
  0.6 36.0 %copy-start = (bf16[512,40]{0,1:T(8,128)(2,1)S(1)}, bf16[512,40]{0,1:T(8,128)(2,1)}, u32[]{:S(2)}) copy-start(bf16[512,40]{0,1:T(8,128)(2,1)} %param.3) | copy-start | bytes 122884
  0.6 35.6 %copy-start.1 = (s32[1024,512]{1,0:T(8,128)S(1)}, s32[1024,512]{1,0:T(8,128)}, u32[]{:S(2)}) copy-start(s32[1024,512]{1,0:T(8,128)} %param.2) | copy-start | bytes 6291460
  100.6 31.8 %copy-start.2 = (bf16[40,1024]{1,0:T(8,128)(2,1)}, bf16[40,1024]{1,0:T(8,128)(2,1)S(1)}, u32[]{:S(2)}) copy-start(bf16[40,1024]{1,0:T(8,128)(2,1)S(1)} %reduce_sum.109) | copy-start | bytes 245764

commit v6 on v5

--- a/solution.py
+++ b/solution.py
@@ -47,8 +47,8 @@
         cut = local.astype(jnp.bfloat16).reshape(-1, SUBLANES, tiles, LANES)
         cut = cut.transpose(0, 2, 1, 3).reshape(members, -1, SUBLANES // 2, LANES)
         part = total_of(exchange(cut, "samp", cell)).astype(jnp.bfloat16)
-        share = (total_of(from_all(part, "samp", stride)) / total).astype(dtype)
-        whole = from_all(share, "samp", cell).reshape(-1, tiles, SUBLANES, LANES)
+        share = (total_of(from_all(part, "samp", stride)) / total).astype(jnp.bfloat16)
+        whole = from_all(share, "samp", cell).astype(dtype).reshape(-1, tiles, SUBLANES, LANES)
         return whole.transpose(0, 2, 1, 3).reshape(rows, width)
 
     def per_device(genotype, basis):

time: 133 us -> 133 us (level)
  no operation moved by 1% of the time
where the time goes in v6:
time: 133 us; the launch traced here: 132 us
  blocking collectives  126 us (95%)
  other arithmetic  3.52 us (3%)
  matrix products  1.38 us (1%)
    all_to_all x10, blocking collectives, exchange(): lax.all_to_all(blocks, axis, split_axis=0, concat_axis=0, tiled=True, axi...  126 us

profile of v6, /device:TPU:1, one launch (start us, length us, event | category | flops | bytes accessed | tf_op | source)
XLA Modules:
  0.0 132.3 jit_solution(6758407313164943124)
XLA Ops:
  0.6 0.0 copy-start
  0.6 0.0 copy-start.1
  0.7 2.1 %select_reduce_fusion = s32[512]{0:T(512)S(1)} fusion(s32[1024,512]{1,0:T(8,128)} %param.2), kind=kLoop, calls=%fused_computation.1 | loop fusion | flops 2096640 | bytes 2099200 | tf_op jit(solution)/shard_map/reduce_sum | solution.py:58
  2.7 12.3 %all_to_all.50 = s32[4,4,128]{2,1,0:T(4,128)S(1)} all-to-all(s32[4,4,128]{2,1,0:T(4,128)S(1)} %broadcast_in_dim.34), channel_id=1, replica_groups={{0,8,256,264},{16,24,272,280},{32,40,288,296},{48,56,304,312},{64,72,32..., dimensions={0} | all-to-all | bytes 16384 | tf_op jit(solution)/shard_map/all_to_all | solution.py:25
  15.1 21.1 %all_to_all.51 = s32[16,4,128]{2,1,0:T(4,128)S(1)} all-to-all(s32[16,4,128]{2,1,0:T(4,128)S(1)} %broadcast_in_dim.35), channel_id=1, replica_groups={{0,16,32,48,64,80,96,112,128,144,160,176,192,208,224,240},{8,24,40,56,7..., dimensions={0} | all-to-all | bytes 65536 | tf_op jit(solution)/shard_map/all_to_all | solution.py:25
  36.2 0.0 copy-done.1
  36.3 0.4 select_convert_fusion
  36.7 0.0 copy-done
  36.7 0.4 fusion
  37.1 0.1 broadcast_in_dim.37
  37.2 16.1 %all_to_all.52 = bf16[8,40,1024]{2,1,0:T(8,128)(2,1)S(1)} all-to-all(bf16[8,40,1024]{2,1,0:T(8,128)(2,1)S(1)} %broadcast_in_dim.37), channel_id=1, replica_groups={{0,2,4,6,7,5,3,1},{8,10,12,14,15,13,11,9},{16,18,20,22,23,21,19,17},{24..., dimensions={0} | all-to-all | bytes 1310720 | tf_op jit(solution)/shard_map/all_to_all | solution.py:25
  53.3 0.1 reduce_sum.106
  53.4 0.3 convolution_convert_fusion.3
  53.7 10.3 %all_to_all.53 = bf16[8,5,4,128]{3,2,1,0:T(4,128)(2,1)S(1)} all-to-all(bf16[8,5,4,128]{3,2,1,0:T(4,128)(2,1)S(1)} %bitcast.44), channel_id=1, replica_groups={{0,8,256,264,16,24,272,280},{32,40,288,296,48,56,304,312},{64,72,320,32..., dimensions={0} | all-to-all | bytes 81920 | tf_op jit(solution)/shard_map/all_to_all | solution.py:25
  64.1 13.0 %all_to_all.54 = bf16[8,5,4,128]{3,2,1,0:T(4,128)(2,1)S(1)} all-to-all(bf16[8,5,4,128]{3,2,1,0:T(4,128)(2,1)S(1)} %broadcast_in_dim.38), channel_id=1, replica_groups={{0,32,64,96,144,176,208,240},{8,40,72,104,152,184,216,248},{256,288,320..., dimensions={0} | all-to-all | bytes 81920 | tf_op jit(solution)/shard_map/all_to_all | solution.py:25
  77.2 9.0 %all_to_all.55 = bf16[8,5,4,128]{3,2,1,0:T(4,128)(2,1)S(1)} all-to-all(bf16[8,5,4,128]{3,2,1,0:T(4,128)(2,1)S(1)} %broadcast_in_dim.39), channel_id=1, replica_groups={{0,8,256,264,16,24,272,280},{32,40,288,296,48,56,304,312},{64,72,320,32..., dimensions={0} | all-to-all | bytes 81920 | tf_op jit(solution)/shard_map/all_to_all | solution.py:25
  86.2 0.4 convolution_convert_fusion
  86.6 0.1 broadcast_in_dim.40
  86.7 13.8 %all_to_all.56 = bf16[8,40,1024]{2,1,0:T(8,128)(2,1)S(1)} all-to-all(bf16[8,40,1024]{2,1,0:T(8,128)(2,1)S(1)} %broadcast_in_dim.40), channel_id=1, replica_groups={{0,2,4,6,7,5,3,1},{8,10,12,14,15,13,11,9},{16,18,20,22,23,21,19,17},{24..., dimensions={0} | all-to-all | bytes 1310720 | tf_op jit(solution)/shard_map/all_to_all | solution.py:25
  100.5 0.1 reduce_sum.109
  100.6 0.0 copy-start.2
  100.6 0.3 convolution_convert_fusion.2
  100.9 8.9 %all_to_all.57 = bf16[8,5,4,128]{3,2,1,0:T(4,128)(2,1)S(1)} all-to-all(bf16[8,5,4,128]{3,2,1,0:T(4,128)(2,1)S(1)} %bitcast.46), channel_id=1, replica_groups={{0,8,256,264,16,24,272,280},{32,40,288,296,48,56,304,312},{64,72,320,32..., dimensions={0} | all-to-all | bytes 81920 | tf_op jit(solution)/shard_map/all_to_all | solution.py:25
  109.8 13.0 %all_to_all.58 = bf16[8,5,4,128]{3,2,1,0:T(4,128)(2,1)S(1)} all-to-all(bf16[8,5,4,128]{3,2,1,0:T(4,128)(2,1)S(1)} %broadcast_in_dim.41), channel_id=1, replica_groups={{0,32,64,96,144,176,208,240},{8,40,72,104,152,184,216,248},{256,288,320..., dimensions={0} | all-to-all | bytes 81920 | tf_op jit(solution)/shard_map/all_to_all | solution.py:25
  122.9 8.7 %all_to_all.59 = bf16[8,5,4,128]{3,2,1,0:T(4,128)(2,1)S(1)} all-to-all(bf16[8,5,4,128]{3,2,1,0:T(4,128)(2,1)S(1)} %broadcast_in_dim.42), channel_id=1, replica_groups={{0,8,256,264,16,24,272,280},{32,40,288,296,48,56,304,312},{64,72,320,32..., dimensions={0} | all-to-all | bytes 81920 | tf_op jit(solution)/shard_map/all_to_all | solution.py:25
  131.7 0.6 convert_bitcast_fusion
  132.3 0.0 copy-done.2
  (16 shorter events, 0.3 us)
Async XLA Ops:
  0.6 36.0 %copy-start = (bf16[512,40]{0,1:T(8,128)(2,1)S(1)}, bf16[512,40]{0,1:T(8,128)(2,1)}, u32[]{:S(2)}) copy-start(bf16[512,40]{0,1:T(8,128)(2,1)} %param.3) | copy-start | bytes 122884
  0.6 35.6 %copy-start.1 = (s32[1024,512]{1,0:T(8,128)S(1)}, s32[1024,512]{1,0:T(8,128)}, u32[]{:S(2)}) copy-start(s32[1024,512]{1,0:T(8,128)} %param.2) | copy-start | bytes 6291460
  100.6 31.7 %copy-start.2 = (bf16[40,1024]{1,0:T(8,128)(2,1)}, bf16[40,1024]{1,0:T(8,128)(2,1)S(1)}, u32[]{:S(2)}) copy-start(bf16[40,1024]{1,0:T(8,128)(2,1)S(1)} %reduce_sum.109) | copy-start | bytes 245764

commit v7 on v6

--- a/solution.py
+++ b/solution.py
@@ -39,7 +39,8 @@
 def solution(mesh):
     level, column, cell, stride = samp_groups(mesh)
     peers = mesh.shape["snp"]
-    snake = [[*range(0, peers, 2), *range(peers - 1, 0, -2)]]
+    pairs = [[k, k + 1] for k in range(0, peers, 2)]
+    lines = [[*range(k, peers, 2)] for k in range(2)]
 
     def block_over_samples(local, total, dtype):
         rows, width = local.shape
@@ -71,7 +72,8 @@
             part = lax.dot_general(
                 block, standard, (((1,), (1,)), ((), ())), preferred_element_type=jnp.float32
             ).astype(jnp.bfloat16)
-            scores = total_of(from_all(part, "snp", snake)).astype(jnp.bfloat16)
+            pair = total_of(lax.all_gather(part, "snp", axis_index_groups=pairs)).astype(jnp.bfloat16)
+            scores = total_of(from_all(pair, "snp", lines)).astype(jnp.bfloat16)
             local = jnp.dot(scores, standard, preferred_element_type=jnp.float32)
             last = step == ITERS - 1
             block = block_over_samples(local, total, jnp.float32 if last else jnp.bfloat16)

time: 133 us -> 133 us (level)
    all_gather x0 -> x2, blocking collectives: none -> 10.9 us  [per_device(): lax.all_gather(part, 'snp', axis_index_groups=pairs)]
    all_to_all x10, blocking collectives: 126 us -> 116 us  [exchange(): lax.all_to_all(blocks, axis, split_axis=0, concat_axis=0, tiled=True, axi...]
where the time goes in v7:
time: 133 us; the launch traced here: 132 us
  blocking collectives  127 us (95%)
  other arithmetic  3.49 us (3%)
  matrix products  1.38 us (1%)
    all_to_all x10, blocking collectives, exchange(): lax.all_to_all(blocks, axis, split_axis=0, concat_axis=0, tiled=True, axi...  116 us
    all_gather x2, blocking collectives, per_device(): lax.all_gather(part, 'snp', axis_index_groups=pairs)  10.9 us

profile of v7, /device:TPU:1, one launch (start us, length us, event | category | flops | bytes accessed | tf_op | source)
XLA Modules:
  0.0 132.4 jit_solution(16856457885420516506)
XLA Ops:
  0.6 0.0 copy-start
  0.6 0.0 copy-start.1
  0.7 2.1 %select_reduce_fusion = s32[512]{0:T(512)S(1)} fusion(s32[1024,512]{1,0:T(8,128)} %param.2), kind=kLoop, calls=%fused_computation.1 | loop fusion | flops 2096640 | bytes 2099200 | tf_op jit(solution)/shard_map/reduce_sum | solution.py:59
  2.7 12.3 %all_to_all.50 = s32[4,4,128]{2,1,0:T(4,128)S(1)} all-to-all(s32[4,4,128]{2,1,0:T(4,128)S(1)} %broadcast_in_dim.34), channel_id=1, replica_groups={{0,8,256,264},{16,24,272,280},{32,40,288,296},{48,56,304,312},{64,72,32..., dimensions={0} | all-to-all | bytes 16384 | tf_op jit(solution)/shard_map/all_to_all | solution.py:25
  15.1 21.1 %all_to_all.51 = s32[16,4,128]{2,1,0:T(4,128)S(1)} all-to-all(s32[16,4,128]{2,1,0:T(4,128)S(1)} %broadcast_in_dim.35), channel_id=1, replica_groups={{0,16,32,48,64,80,96,112,128,144,160,176,192,208,224,240},{8,24,40,56,7..., dimensions={0} | all-to-all | bytes 65536 | tf_op jit(solution)/shard_map/all_to_all | solution.py:25
  36.2 0.0 copy-done.1
  36.3 0.4 select_convert_fusion
  36.7 0.0 copy-done
  36.7 0.4 fusion
  37.1 5.5 %all-gather = bf16[80,1024]{1,0:T(8,128)(2,1)S(1)} all-gather(bf16[40,1024]{1,0:T(8,128)(2,1)S(1)} %fusion), channel_id=2, replica_groups={{0,1},{2,3},{4,5},{6,7},{8,9},{10,11},{12,13},{14,15},{16,17},{18,19},{..., dimensions={0}, use_global_device_ids=true | all-gather | bytes 245760 | tf_op jit(solution)/shard_map/all_gather | solution.py:75
  42.6 9.7 %all_to_all.52 = bf16[4,40,1024]{2,1,0:T(8,128)(2,1)S(1)} all-to-all(bf16[4,40,1024]{2,1,0:T(8,128)(2,1)S(1)} %broadcast_in_dim.37), channel_id=1, replica_groups={{0,2,4,6},{1,3,5,7},{8,10,12,14},{9,11,13,15},{16,18,20,22},{17,19,21,2..., dimensions={0} | all-to-all | bytes 655360 | tf_op jit(solution)/shard_map/all_to_all | solution.py:25
  52.3 0.1 reduce_sum.131
  52.4 0.3 convolution_convert_fusion.3
  52.7 11.1 %all_to_all.53 = bf16[8,5,4,128]{3,2,1,0:T(4,128)(2,1)S(1)} all-to-all(bf16[8,5,4,128]{3,2,1,0:T(4,128)(2,1)S(1)} %bitcast.48), channel_id=1, replica_groups={{0,8,256,264,16,24,272,280},{32,40,288,296,48,56,304,312},{64,72,320,32..., dimensions={0} | all-to-all | bytes 81920 | tf_op jit(solution)/shard_map/all_to_all | solution.py:25
  63.8 13.0 %all_to_all.54 = bf16[8,5,4,128]{3,2,1,0:T(4,128)(2,1)S(1)} all-to-all(bf16[8,5,4,128]{3,2,1,0:T(4,128)(2,1)S(1)} %broadcast_in_dim.38), channel_id=1, replica_groups={{0,32,64,96,144,176,208,240},{8,40,72,104,152,184,216,248},{256,288,320..., dimensions={0} | all-to-all | bytes 81920 | tf_op jit(solution)/shard_map/all_to_all | solution.py:25
  76.9 8.8 %all_to_all.55 = bf16[8,5,4,128]{3,2,1,0:T(4,128)(2,1)S(1)} all-to-all(bf16[8,5,4,128]{3,2,1,0:T(4,128)(2,1)S(1)} %broadcast_in_dim.39), channel_id=1, replica_groups={{0,8,256,264,16,24,272,280},{32,40,288,296,48,56,304,312},{64,72,320,32..., dimensions={0} | all-to-all | bytes 81920 | tf_op jit(solution)/shard_map/all_to_all | solution.py:25
  85.7 0.4 convolution_convert_fusion
  86.1 5.5 %all-gather.1 = bf16[80,1024]{1,0:T(8,128)(2,1)S(1)} all-gather(bf16[40,1024]{1,0:T(8,128)(2,1)S(1)} %convolution_convert_fusion), channel_id=3, replica_groups={{0,1},{2,3},{4,5},{6,7},{8,9},{10,11},{12,13},{14,15},{16,17},{18,19},{..., dimensions={0}, use_global_device_ids=true | all-gather | bytes 245760 | tf_op jit(solution)/shard_map/all_gather | solution.py:75
  91.6 8.3 %all_to_all.56 = bf16[4,40,1024]{2,1,0:T(8,128)(2,1)S(1)} all-to-all(bf16[4,40,1024]{2,1,0:T(8,128)(2,1)S(1)} %broadcast_in_dim.40), channel_id=1, replica_groups={{0,2,4,6},{1,3,5,7},{8,10,12,14},{9,11,13,15},{16,18,20,22},{17,19,21,2..., dimensions={0} | all-to-all | bytes 655360 | tf_op jit(solution)/shard_map/all_to_all | solution.py:25
  99.9 0.1 reduce_sum.135
  99.9 0.0 copy-start.2
  100.0 0.3 convolution_convert_fusion.2
  100.2 9.5 %all_to_all.57 = bf16[8,5,4,128]{3,2,1,0:T(4,128)(2,1)S(1)} all-to-all(bf16[8,5,4,128]{3,2,1,0:T(4,128)(2,1)S(1)} %bitcast.50), channel_id=1, replica_groups={{0,8,256,264,16,24,272,280},{32,40,288,296,48,56,304,312},{64,72,320,32..., dimensions={0} | all-to-all | bytes 81920 | tf_op jit(solution)/shard_map/all_to_all | solution.py:25
  109.7 13.1 %all_to_all.58 = bf16[8,5,4,128]{3,2,1,0:T(4,128)(2,1)S(1)} all-to-all(bf16[8,5,4,128]{3,2,1,0:T(4,128)(2,1)S(1)} %broadcast_in_dim.41), channel_id=1, replica_groups={{0,32,64,96,144,176,208,240},{8,40,72,104,152,184,216,248},{256,288,320..., dimensions={0} | all-to-all | bytes 81920 | tf_op jit(solution)/shard_map/all_to_all | solution.py:25
  122.9 8.9 %all_to_all.59 = bf16[8,5,4,128]{3,2,1,0:T(4,128)(2,1)S(1)} all-to-all(bf16[8,5,4,128]{3,2,1,0:T(4,128)(2,1)S(1)} %broadcast_in_dim.42), channel_id=1, replica_groups={{0,8,256,264,16,24,272,280},{32,40,288,296,48,56,304,312},{64,72,320,32..., dimensions={0} | all-to-all | bytes 81920 | tf_op jit(solution)/shard_map/all_to_all | solution.py:25
  131.8 0.6 convert_bitcast_fusion
  132.4 0.0 copy-done.2
  (20 shorter events, 0.4 us)
Async XLA Ops:
  0.6 36.0 %copy-start = (bf16[512,40]{0,1:T(8,128)(2,1)S(1)}, bf16[512,40]{0,1:T(8,128)(2,1)}, u32[]{:S(2)}) copy-start(bf16[512,40]{0,1:T(8,128)(2,1)} %param.3) | copy-start | bytes 122884
  0.6 35.6 %copy-start.1 = (s32[1024,512]{1,0:T(8,128)S(1)}, s32[1024,512]{1,0:T(8,128)}, u32[]{:S(2)}) copy-start(s32[1024,512]{1,0:T(8,128)} %param.2) | copy-start | bytes 6291460
  99.9 32.5 %copy-start.2 = (bf16[40,1024]{1,0:T(8,128)(2,1)}, bf16[40,1024]{1,0:T(8,128)(2,1)S(1)}, u32[]{:S(2)}) copy-start(bf16[40,1024]{1,0:T(8,128)(2,1)S(1)} %reduce_sum.135) | copy-start | bytes 245764
